TPU v7x, 32 devices: a whole 2x2x4 slice. The times are simulated.
32 devices in a mesh: date: 8 (over y, x, core), rng: 4 (over z).
Axes of the slice: x: 2, y: 2, z: 4, core: 2. Of those that a mesh axis runs over, the one named last changes fastest.
Arguments:
- slc_re: bfloat16 [8, 2048, 512], P('date', None, 'rng'), may hold values from -170 to 170
- slc_im: bfloat16 [8, 2048, 512], P('date', None, 'rng'), may hold values from -170 to 170
- ref_date: int32 [1], replicated, may hold values from 0 to 7
- gain: float32 [2048], replicated, may hold values from 0.25 to 2
- bperp: int32 [8], replicated, may hold values from -200 to 199
- tdays: int32 [8], replicated, may hold values from 0 to 1899
- mask: int32 [2048, 512], P(None, 'rng'), may hold values from 0 to 1, as said below
Outputs:
- periodogram: float32 [2048, 512, 256], P('date', 'rng')
Inputs may be any that keep to these rules, and one draw needn't show every extreme that they name: `mask`: each aligned block of 256 lines by 128 range columns holds exactly 8192 candidates.
All inputs are finite; a program needn't handle non-finite values.
Results may differ from a plain program's by a relative error of at most 0.0067.
Values may be sent and summed in bfloat16 or wider, within the bound.
A program may use at most 192 MiB of HBM per device.

v0:
```python
import math

import jax
import jax.numpy as jnp
from jax import lax
from jax.sharding import PartitionSpec as P

HGRID = 16
VGRID = 16
PHASE_Q = 1024


def broadcast(shard, axis, root):
    mine = lax.axis_index(axis) == root
    return lax.psum(jnp.where(mine, shard, jnp.zeros_like(shard)), axis)


def dft_tables(length):
    positions = jnp.arange(length, dtype=jnp.int32)
    products = positions[:, None] * positions[None, :] % length
    angles = products.astype(jnp.float32) * (2.0 * math.pi / length)
    return (jnp.cos(angles).astype(jnp.bfloat16), jnp.sin(angles).astype(jnp.bfloat16))


def phase_tables(bperp, tdays):
    grid_points = jnp.arange(HGRID * VGRID, dtype=jnp.int32)
    height_step = grid_points // VGRID
    speed_step = grid_points % VGRID
    quanta = (
        bperp[:, None] * height_step[None, :] + tdays[:, None] * speed_step[None, :]
    ) % PHASE_Q
    angles = quanta.astype(jnp.float32) * (2.0 * math.pi / PHASE_Q)
    phase_re = jnp.cos(angles).astype(jnp.bfloat16)
    phase_im = jnp.sin(angles).astype(jnp.bfloat16)
    upper = jnp.concatenate([phase_re, -phase_im], axis=1)
    lower = jnp.concatenate([phase_im, phase_re], axis=1)
    return jnp.concatenate([upper, lower], axis=0)


def coherence_map(piece_re, piece_im, phase_table):
    date_count = piece_re.shape[0]
    grid_size = phase_table.shape[1] // 2
    stacked = jnp.concatenate([piece_re, piece_im], axis=0)
    spectra = lax.dot_general(
        stacked, phase_table, (((0,), (0,)), ((), ())), preferred_element_type=jnp.float32
    )
    peri_re = spectra[:, :grid_size]
    peri_im = spectra[:, grid_size:]
    wide_re = piece_re.astype(jnp.float32)
    wide_im = piece_im.astype(jnp.float32)
    pixel_power = jnp.sum(wide_re * wide_re + wide_im * wide_im, axis=0) / date_count
    return (peri_re * peri_re + peri_im * peri_im) / (date_count * jnp.maximum(pixel_power, 1.0))[
        :, None
    ]


def shards(slc_re, slc_im, ref_date, gain, bperp, tdays, mask):
    date_dev, lines, rg_dev = slc_re.shape
    date_axis = lax.axis_size("date")
    pixel_total = lines * rg_dev * lax.axis_size("rng")
    ref_index = ref_date[0]
    owner_index = ref_index // date_dev
    owner_slot = ref_index % date_dev
    own_re = lax.dynamic_index_in_dim(slc_re, owner_slot, 0, keepdims=False)
    own_im = lax.dynamic_index_in_dim(slc_im, owner_slot, 0, keepdims=False)
    ref_re, ref_im = (
        broadcast(own_re, "date", owner_index),
        broadcast(own_im, "date", owner_index),
    )
    wide_re = slc_re.astype(jnp.float32)
    wide_im = slc_im.astype(jnp.float32)
    ref_wide_re = ref_re.astype(jnp.float32)
    ref_wide_im = ref_im.astype(jnp.float32)
    local_sums = jnp.sum(wide_re * wide_re + wide_im * wide_im, axis=(1, 2))
    ref_local = jnp.sum(ref_wide_re * ref_wide_re + ref_wide_im * ref_wide_im)
    date_sums, ref_sum = lax.psum((local_sums, ref_local), "rng")
    scales = lax.rsqrt(date_sums / pixel_total + 1e-06)
    ref_scale = lax.rsqrt(ref_sum / pixel_total + 1e-06)
    own_part_re = wide_re * scales[:, None, None]
    own_part_im = wide_im * scales[:, None, None]
    ref_part_re = (ref_wide_re * ref_scale)[None]
    ref_part_im = (ref_wide_im * ref_scale)[None]
    ifg_re = (own_part_re * ref_part_re + own_part_im * ref_part_im).astype(jnp.bfloat16)
    ifg_im = (own_part_im * ref_part_re - own_part_re * ref_part_im).astype(jnp.bfloat16)
    cos_table, sin_table = dft_tables(lines)
    pair = jnp.stack([ifg_re, ifg_im])
    cos_part = jnp.einsum("fl,kdlc->kdfc", cos_table, pair, preferred_element_type=jnp.float32)
    sin_part = jnp.einsum("fl,kdlc->kdfc", sin_table, pair, preferred_element_type=jnp.float32)
    spec_re = cos_part[0] + sin_part[1]
    spec_im = cos_part[1] - sin_part[0]
    weights = gain[:, None]
    held = jnp.stack(
        [(spec_re * weights).astype(jnp.bfloat16), (spec_im * weights).astype(jnp.bfloat16)]
    )
    back_cos = jnp.einsum("fl,kdfc->kdlc", cos_table, held, preferred_element_type=jnp.float32)
    back_sin = jnp.einsum("fl,kdfc->kdlc", sin_table, held, preferred_element_type=jnp.float32)
    filt_re = ((back_cos[0] - back_sin[1]) * (1.0 / lines)).astype(jnp.bfloat16)
    filt_im = ((back_sin[0] + back_cos[1]) * (1.0 / lines)).astype(jnp.bfloat16)
    phase_table = phase_tables(bperp, tdays)
    grid_size = HGRID * VGRID
    lines_dev = lines // date_axis
    my_index = lax.axis_index("date")
    piece_re = lax.all_to_all(filt_re, "date", split_axis=1, concat_axis=0, tiled=True)
    piece_im = lax.all_to_all(filt_im, "date", split_axis=1, concat_axis=0, tiled=True)
    row_count = piece_re.shape[1]
    col_count = piece_re.shape[2]
    flat_re = piece_re.reshape(piece_re.shape[0], row_count * col_count)
    flat_im = piece_im.reshape(piece_im.shape[0], row_count * col_count)
    result = coherence_map(flat_re, flat_im, phase_table)
    mapped = result.reshape(row_count, col_count, grid_size)
    mask_rows = lax.dynamic_slice_in_dim(mask, my_index * lines_dev, lines_dev, 0)
    return mapped * mask_rows.astype(jnp.float32)[:, :, None]


def solution(mesh):
    in_specs = (P("date", None, "rng"), P("date", None, "rng"), P(), P(), P(), P(), P(None, "rng"))
    out_specs = P("date", "rng", None)
    return jax.shard_map(shards, mesh=mesh, in_specs=in_specs, out_specs=out_specs, check_vma=False)
```

profile of v0, /device:TPU:3, one launch (start us, length us, event | category | flops | bytes accessed | tf_op | source)
XLA Modules:
  0.0 487.4 jit_solution(7658852698943665809)
XLA Ops:
  6.5 0.0 all-reduce.4.cloned.1.call-start
  6.5 1.2 copy.20
  7.8 1.2 copy.21
  9.7 1.1 select_bitcast_fusion
  10.8 0.0 all-reduce.4.cloned.1.call-update
  10.8 0.9 fusion.39
  11.7 55.3 %all-reduce.4.cloned.1.call-done = (bf16[2048,128]{0,1:T(8,128)(2,1)}, bf16[2048,128]{0,1:T(8,128)(2,1)}) async-done(((bf16[2048,128]{0,1:T(8,128)(2,1)}, bf16[2048,128]{0,1:T(8,128)(2,1)}), (bf16[2048,128]{0,1:T(8,128)(2,1)}, bf16[2048,128]{0,1:T(8,128)(2,1)})) %all-reduce.4.cloned.1.call-update) | async-done | bytes 1048592 | tf_op jit(solution)/shard_map/psum | solution.py:15
  67.0 2.1 fusion.41
  69.1 10.2 %all-reduce = (f32[]{:T(128)}, f32[1]{0:T(128)}) all-reduce(f32[]{:T(128)} %fusion.41, f32[1]{0:T(128)} %bitcast), channel_id=1, replica_groups=mesh['date'=8,'rng'=4] {'rng'}, use_global_device_ids=true, to_apply=%region_5.6 | all-reduce | flops 2 | bytes 16 | tf_op jit(solution)/shard_map/psum | solution.py:76
  80.7 1.7 fusion.59
  82.4 0.1 maximum_bitcast_fusion.18
  82.5 0.1 maximum_bitcast_fusion.20
  82.6 63.5 %fusion.18 = f32[2,1,2048,128]{2,3,0,1:T(8,128)S(1)} fusion(bf16[2,2048,128]{1,2,0:T(8,128)(2,1)S(1)} %maximum_bitcast_fusion.18), kind=kOutput, calls=%fused_computation.22 | convolution fusion | flops 2210398208 | bytes 3145728 | tf_op jit(solution)/shard_map/fl,kdlc->kdfc/dot_general | solution.py:87
  146.1 0.0 copy-start
  146.1 64.0 %fusion.24 = f32[2,1,2048,128]{2,3,0,1:T(8,128)S(1)} fusion(bf16[2,2048,128]{1,2,0:T(8,128)(2,1)S(1)} %maximum_bitcast_fusion.20), kind=kOutput, calls=%fused_computation.24 | convolution fusion | flops 2210398208 | bytes 3145728 | tf_op jit(solution)/shard_map/fl,kdlc->kdfc/dot_general | solution.py:88
  210.2 0.0 copy-done
  210.2 0.4 fusion.51
  210.6 0.1 maximum_bitcast_fusion.19
  210.7 0.1 maximum_bitcast_fusion.21
  210.8 63.2 %fusion.21 = f32[2,1,2048,128]{2,3,0,1:T(8,128)S(1)} fusion(bf16[2,2048,128]{1,2,0:T(8,128)(2,1)S(1)} %maximum_bitcast_fusion.19), kind=kOutput, calls=%fused_computation.23 | convolution fusion | flops 2210398208 | bytes 3145728 | tf_op jit(solution)/shard_map/fl,kdfc->kdlc/dot_general | solution.py:95
  274.0 0.0 copy-start.1
  274.0 0.0 copy-start.2
  274.0 63.5 %fusion.27 = f32[2,1,2048,128]{2,3,0,1:T(8,128)S(1)} fusion(bf16[2,2048,128]{1,2,0:T(8,128)(2,1)S(1)} %maximum_bitcast_fusion.21), kind=kOutput, calls=%fused_computation.25 | convolution fusion | flops 2210398208 | bytes 3145728 | tf_op jit(solution)/shard_map/fl,kdfc->kdlc/dot_general | solution.py:96
  337.5 0.4 fusion.56
  338.0 0.8 copy.25
  338.7 0.5 broadcast.173
  339.2 11.7 %reduce.6 = bf16[2048,128]{1,0:T(8,128)(2,1)S(1)} reduce(bf16[2048,1,128]{2,1,0:T(2,128)(2,1)S(1)} %bitcast.126, bf16[]{:T(256)} %broadcast.173), dimensions={1}, to_apply=%bitcast.80.reduce_sub_computation | reduce | bytes 1048578
  351.0 0.9 reshape.172
  351.9 8.2 %all-to-all-start = ((bf16[8,2,16384]{2,1,0:T(2,128)(2,1)}), bf16[8,2,16384]{2,1,0:T(2,128)(2,1)S(1)}, u32[]{:S(2)}, u32[]{:S(2)}) async-start(bf16[8,2,16384]{2,1,0:T(2,128)(2,1)} %reshape.172), calls=%async_computation | async-start | bytes 1048576 | tf_op jit(solution)/shard_map/all_to_all | solution.py:103
  360.1 0.9 dynamic-slice_convert_fusion
  361.0 0.0 copy-done.1
  361.0 0.0 copy-done.2
  361.0 0.1 sine_convert_fusion.1
  361.2 0.8 copy.26
  361.9 11.5 %reduce.5 = bf16[2048,128]{1,0:T(8,128)(2,1)S(1)} reduce(bf16[2048,1,128]{2,1,0:T(2,128)(2,1)S(1)} %bitcast.127, bf16[]{:T(256)} %broadcast.173), dimensions={1}, to_apply=%bitcast.78.reduce_sub_computation | reduce | bytes 1048578
  373.5 0.9 reshape.170
  374.4 0.0 all-to-all-done
  374.4 4.5 all-to-all-start.1
  378.9 0.1 fusion.93
  379.0 0.5 reshape.173
  379.6 8.8 %bitcast_reduce_fusion = bf16[2048,128]{1,0:T(8,128)(2,1)S(1)} fusion(bf16[2048,1,128]{2,1,0:T(2,128)(2,1)S(1)} %reshape.173), kind=kLoop, calls=%fused_computation.119 | loop fusion | bytes 1048576 | tf_op jit(solution)/shard_map/all_to_all | solution.py:103
  388.3 0.2 reshape.163
  388.6 0.0 all-to-all-done.1
  388.6 0.5 reshape.171
  389.1 8.8 %bitcast_reduce_fusion.1 = bf16[2048,128]{1,0:T(8,128)(2,1)S(1)} fusion(bf16[2048,1,128]{2,1,0:T(2,128)(2,1)S(1)} %reshape.171), kind=kLoop, calls=%fused_computation.120 | loop fusion | bytes 1048576 | tf_op jit(solution)/shard_map/all_to_all | solution.py:104
  397.9 0.2 reshape.164
  398.1 0.4 add_reduce_fusion
  398.6 24.3 %fusion.52 = f32[32768,512]{1,0:T(8,128)} fusion(bf16[8,32768]{1,0:T(8,128)(2,1)S(1)} %reshape.164, bf16[8,32768]{1,0:T(8,128)(2,1)S(1)} %reshape.163, bf16[8,256]{1,0:T(8,128)(2,1)S(1)} %get-tuple-element.16, bf16[8,256]{1,0:T(8,128)(2,1)S(1)} %get-tuple-element.15, bf16[8,256]{1,0:T(8,128)(2,1)S(1)} %fusion.93), kind=kOutput, calls=%fused_computation.62 | convolution fusion | flops 539033600 | bytes 68169728 | tf_op jit(solution)/shard_map/dot_general | solution.py:44
  422.9 33.6 %fusion.1 = f32[32768,256]{1,0:T(8,128)} fusion(f32[32768,512]{1,0:T(8,128)} %fusion.52, f32[32768]{0:T(1024)S(1)} %maximum_multiply_fusion), kind=kLoop, calls=%fused_computation.2 | loop fusion | flops 33554432 | bytes 100794368 | tf_op jit(solution)/shard_map/div | solution.py:52
  456.5 23.6 %broadcast_multiply_fusion = f32[256,128,256]{2,1,0:T(8,128)} fusion(f32[256,128,256]{2,1,0:T(8,128)} %bitcast.125, f32[256,128]{1,0:T(8,128)S(1)} %dynamic-slice_convert_fusion), kind=kLoop, calls=%fused_computation.10 | loop fusion | flops 8388608 | bytes 67239936 | tf_op jit(solution)/shard_map/mul | solution.py:112
  (2 shorter events, 0.0 us)
Async XLA Ops:
  6.5 60.4 %all-reduce.4.cloned.1.call-start = ((), (), s32[]{:S(2)}) async-start(), calls=%async_computation.2 | async-start | bytes 2097152 | tf_op jit(solution)/shard_map/psum | solution.py:15
  146.1 64.1 %copy-start = (f32[2048]{0:T(1024)S(1)}, f32[2048]{0:T(1024)}, u32[]{:S(2)}) copy-start(f32[2048]{0:T(1024)} %param.10) | copy-start | bytes 24580
  274.0 87.0 %copy-start.1 = (s32[8]{0:T(128)S(1)}, s32[8]{0:T(128)}, u32[]{:S(2)}) copy-start(s32[8]{0:T(128)} %param.12) | copy-start | bytes 100
  274.0 87.0 %copy-start.2 = (s32[8]{0:T(128)S(1)}, s32[8]{0:T(128)}, u32[]{:S(2)}) copy-start(s32[8]{0:T(128)} %param.11) | copy-start | bytes 100
  351.9 22.5 %all-to-all-start = ((bf16[8,2,16384]{2,1,0:T(2,128)(2,1)}), bf16[8,2,16384]{2,1,0:T(2,128)(2,1)S(1)}, u32[]{:S(2)}, u32[]{:S(2)}) async-start(bf16[8,2,16384]{2,1,0:T(2,128)(2,1)} %reshape.172), calls=%async_computation | async-start | bytes 1048576 | tf_op jit(solution)/shard_map/all_to_all | solution.py:103
  374.4 14.2 %all-to-all-start.1 = ((bf16[8,2,16384]{2,1,0:T(2,128)(2,1)}), bf16[8,2,16384]{2,1,0:T(2,128)(2,1)S(1)}, u32[]{:S(2)}, u32[]{:S(2)}) async-start(bf16[8,2,16384]{2,1,0:T(2,128)(2,1)} %reshape.170), calls=%async_computation.1 | async-start | bytes 1048576 | tf_op jit(solution)/shard_map/all_to_all | solution.py:104
Sparse Core Ops, SparseCore 0:
  10.9 56.0 all-reduce.3
where the time goes:
time: 496 us; the launch traced here: 487 us
  matrix products  279 us (56%)
  other arithmetic  89 us (18%)
  waiting for transfers between devices  55.3 us (11%)
  local copies, waits for them, and re-layouts  25.4 us (5%)
  between operations  16.2 us (3%)
  starting transfers between devices  12.7 us (3%)
  blocking collectives  10.2 us (2%)
    dot_general x1, matrix products, shards(): jnp.einsum('fl,kdlc->kdfc', sin_table, pair, preferred_element_type=jnp.f...  64 us
    dot_general x1, matrix products, shards(): jnp.einsum('fl,kdfc->kdlc', sin_table, held, preferred_element_type=jnp.f...  63.5 us
    dot_general x1, matrix products, shards(): jnp.einsum('fl,kdlc->kdfc', cos_table, pair, preferred_element_type=jnp.f...  63.5 us
    dot_general x1, matrix products, shards(): jnp.einsum('fl,kdfc->kdlc', cos_table, held, preferred_element_type=jnp.f...  63.2 us
    psum x1, waiting for transfers between devices, broadcast(): return lax.psum(jnp.where(mine, shard, jnp.zeros_like(shard)), axis)  55.3 us
    div x1, other arithmetic, coherence_map(): (peri_re * peri_re + peri_im * peri_im) / (date_count * jnp.maximum(pixel...  33.6 us
    dot_general x1, matrix products, coherence_map(): lax.dot_general(stacked, phase_table, (((0,), (0,)), ((), ())), preferred...  24.3 us
    mul x1, other arithmetic, shards(): return mapped * mask_rows.astype(jnp.float32)[:, :, None]  23.6 us
  transfers between devices with their start and end apart: 3, of which 1 were waited for; matrix products, arithmetic and copies ran while one was open for 5% of the time, Pallas kernels for 0%

commit v1 on v0

v1 whole, which is shorter than its diff:
```python
import functools
import math

import jax
import jax.numpy as jnp
import ml_dtypes
import numpy as np
from jax import lax
from jax.experimental import pallas as pl
from jax.experimental.pallas import tpu as pltpu
from jax.sharding import PartitionSpec as P

HGRID = 16
VGRID = 16
PHASE_Q = 1024
RADIX = 16
ROWS = 16
MESH = pl.DeviceIdType.MESH
VMEM_BYTES = 56 * 1024 * 1024


def broadcast(shard, axis, root):
    mine = lax.axis_index(axis) == root
    return lax.psum(jnp.where(mine, shard, jnp.zeros_like(shard)), axis)


def dft_blocks(length):
    depth = length // RADIX
    first = np.arange(RADIX)[:, None, None]
    freq = first + RADIX * np.arange(depth)[None, :, None]
    line = np.arange(depth)[None, None, :]
    angle = (freq * line % length) * (2.0 * math.pi / length)
    cos, sin = np.cos(angle), np.sin(angle)
    forward = np.concatenate(
        [np.concatenate([cos, sin], axis=2), np.concatenate([-sin, cos], axis=2)], axis=1
    )
    backward = np.transpose(forward, (0, 2, 1)) / length
    return forward.astype(ml_dtypes.bfloat16), backward.astype(ml_dtypes.bfloat16)


def phase_table(bperp, tdays):
    grid_points = jnp.arange(HGRID * VGRID, dtype=jnp.int32)
    height_step = grid_points // VGRID
    speed_step = grid_points % VGRID
    quanta = (
        bperp[:, None] * height_step[None, :] + tdays[:, None] * speed_step[None, :]
    ) % PHASE_Q
    angles = quanta.astype(jnp.float32) * (2.0 * math.pi / PHASE_Q)
    phase_re = jnp.cos(angles)
    phase_im = jnp.sin(angles)
    upper = jnp.concatenate([phase_re, -phase_im], axis=1)
    lower = jnp.concatenate([phase_im, phase_re], axis=1)
    return jnp.stack([upper, lower], axis=1).reshape(-1, 2 * HGRID * VGRID)


def radix4(a, b, c, d, sign):
    sum_re, sum_im = a[0] + c[0], a[1] + c[1]
    dif_re, dif_im = a[0] - c[0], a[1] - c[1]
    other_re, other_im = b[0] + d[0], b[1] + d[1]
    turn_re, turn_im = b[0] - d[0], b[1] - d[1]
    if sign > 0:
        turn_re, turn_im = -turn_im, turn_re
    else:
        turn_re, turn_im = turn_im, -turn_re
    return (
        (sum_re + other_re, sum_im + other_im),
        (dif_re + turn_re, dif_im + turn_im),
        (sum_re - other_re, sum_im - other_im),
        (dif_re - turn_re, dif_im - turn_im),
    )


def twiddle(value, power, sign):
    power %= 16
    if power == 0:
        return value
    re, im = value
    if power == 4:
        return (-im, re) if sign > 0 else (im, -re)
    if power == 2:
        half = math.sqrt(0.5)
        if sign > 0:
            return ((re - im) * half, (re + im) * half)
        return ((re + im) * half, (im - re) * half)
    if power == 6:
        half = math.sqrt(0.5)
        if sign > 0:
            return ((re + im) * -half, (re - im) * half)
        return ((im - re) * half, (re + im) * -half)
    angle = sign * 2.0 * math.pi * power / 16
    cos, sin = math.cos(angle), math.sin(angle)
    return (re * cos - im * sin, re * sin + im * cos)


def dft16(values, sign):
    inner = [radix4(*[values[4 * n1 + n2] for n1 in range(4)], sign) for n2 in range(4)]
    out = [None] * 16
    for k1 in range(4):
        column = [twiddle(inner[n2][k1], n2 * k1, sign) for n2 in range(4)]
        for k2, value in enumerate(radix4(*column, sign)):
            out[k1 + 4 * k2] = value
    return out


def filter_kernel(
    dates, ranges, re_ref, im_ref, ref_re_ref, ref_im_ref, gain_ref, fwd_ref, inv_ref,
    out_ref, spec, back, filt, sums, peer_sums,
    sum_send, sum_recv, send_sem, recv_sem, own_sem,
):
    date = lax.axis_index("date")
    rng = lax.axis_index("rng")
    lines = re_ref.shape[0]
    depth = lines // RADIX
    lines_dev = lines // dates
    pixels = lines * re_ref.shape[1] * ranges

    barrier = pltpu.get_barrier_semaphore()

    def greet(step, carry):
        other = lax.rem(date + step, dates)
        pl.semaphore_signal(barrier, inc=1, device_id=(other, rng), device_id_type=MESH)
        return carry

    lax.fori_loop(1, dates, greet, 0)
    for step in range(1, ranges):
        other = lax.rem(rng + step, ranges)
        pl.semaphore_signal(barrier, inc=1, device_id=(date, other), device_id_type=MESH)

    for k, (a_ref, b_ref) in enumerate(((re_ref, im_ref), (ref_re_ref, ref_im_ref))):
        def add(i, total, a_ref=a_ref, b_ref=b_ref):
            rows = pl.ds(pl.multiple_of(i * 128, 128), 128)
            a = a_ref[rows, :].astype(jnp.float32)
            b = b_ref[rows, :].astype(jnp.float32)
            return total + jnp.sum((a * a + b * b).reshape(16, 8, 128), axis=0)

        sums[k] = lax.fori_loop(0, lines // 128, add, jnp.zeros((8, 128), jnp.float32))

    pl.semaphore_wait(barrier, dates - 1 + ranges - 1)
    sum_copies = []
    for step in range(1, ranges):
        other = lax.rem(rng + step, ranges)
        copy = pltpu.make_async_remote_copy(
            src_ref=sums, dst_ref=peer_sums.at[step - 1],
            send_sem=sum_send.at[step - 1], recv_sem=sum_recv.at[step - 1],
            device_id=(date, other), device_id_type=MESH,
        )
        copy.start()
        sum_copies.append(copy)
    for copy in sum_copies:
        copy.wait()
    total = sums[...]
    for step in range(1, ranges):
        total = total + peer_sums[step - 1]
    power = jnp.sum(total, axis=(1, 2), keepdims=True) * (1.0 / pixels)
    scale = lax.rsqrt(power + 1e-06)
    own_scale, ref_scale = scale[0], scale[1]

    def forward(q, carry):
        values = []
        for l1 in range(RADIX):
            rows = pl.ds(pl.multiple_of(l1 * depth + q * ROWS, ROWS), ROWS)
            own_re = re_ref[rows, :].astype(jnp.float32) * own_scale
            own_im = im_ref[rows, :].astype(jnp.float32) * own_scale
            ref_re = ref_re_ref[rows, :].astype(jnp.float32) * ref_scale
            ref_im = ref_im_ref[rows, :].astype(jnp.float32) * ref_scale
            ifg_re = (own_re * ref_re + own_im * ref_im).astype(jnp.bfloat16)
            ifg_im = (own_im * ref_re - own_re * ref_im).astype(jnp.bfloat16)
            values.append((ifg_re.astype(jnp.float32), ifg_im.astype(jnp.float32)))
        for f1, (re, im) in enumerate(dft16(values, -1)):
            spec[f1, pl.ds(pl.multiple_of(q * ROWS, ROWS), ROWS), :] = re.astype(jnp.bfloat16)
            spec[f1, pl.ds(pl.multiple_of(depth + q * ROWS, ROWS), ROWS), :] = im.astype(
                jnp.bfloat16
            )
        return carry

    lax.fori_loop(0, depth // ROWS, forward, 0)

    def band(f1, carry):
        spectrum = jnp.dot(fwd_ref[f1], spec[f1], preferred_element_type=jnp.float32)
        weight = gain_ref[f1]
        weighted = jnp.concatenate([spectrum[:depth] * weight, spectrum[depth:] * weight], axis=0)
        back[f1] = jnp.dot(
            inv_ref[f1], weighted.astype(jnp.bfloat16), preferred_element_type=jnp.float32
        )
        return carry

    lax.fori_loop(0, RADIX, band, 0, unroll=4)

    def inverse(q, carry):
        top = pl.ds(pl.multiple_of(q * ROWS, ROWS), ROWS)
        low = pl.ds(pl.multiple_of(depth + q * ROWS, ROWS), ROWS)
        values = [(back[f1, top, :], back[f1, low, :]) for f1 in range(RADIX)]
        for l1, (re, im) in enumerate(dft16(values, 1)):
            rows = pl.ds(pl.multiple_of(l1 * depth + q * ROWS, ROWS), ROWS)
            filt[0, rows, :] = re.astype(jnp.bfloat16)
            filt[1, rows, :] = im.astype(jnp.bfloat16)
        return carry

    lax.fori_loop(0, depth // ROWS, inverse, 0)

    def block(owner):
        return filt.at[:, pl.ds(pl.multiple_of(owner * lines_dev, ROWS), lines_dev), :]

    def piece(step):
        other = lax.rem(date + step, dates)
        return pltpu.make_async_remote_copy(
            src_ref=block(other), dst_ref=out_ref.at[date],
            send_sem=send_sem.at[step - 1], recv_sem=recv_sem.at[step - 1],
            device_id=(other, rng), device_id_type=MESH,
        )

    def send(step, carry):
        piece(step).start()
        return carry

    def finish(step, carry):
        piece(step).wait()
        return carry

    own = pltpu.make_async_copy(block(date), out_ref.at[date], own_sem)
    lax.fori_loop(1, dates, send, 0)
    own.start()
    own.wait()
    lax.fori_loop(1, dates, finish, 0)


def filtered_pieces(dates, ranges, re, im, ref_re, ref_im, gain):
    lines, columns = re.shape
    depth = lines // RADIX
    lines_dev = lines // dates
    fwd, inv = dft_blocks(lines)
    weights = jnp.broadcast_to(gain.reshape(depth, RADIX).T[:, :, None], (RADIX, depth, columns))
    vmem = pl.BlockSpec(memory_space=pltpu.VMEM)
    return pl.pallas_call(
        functools.partial(filter_kernel, dates, ranges),
        out_shape=jax.ShapeDtypeStruct((dates, 2, lines_dev, columns), jnp.bfloat16),
        in_specs=[vmem] * 7,
        out_specs=pl.BlockSpec(memory_space=pl.ANY),
        scratch_shapes=[
            pltpu.VMEM((RADIX, 2 * depth, columns), jnp.bfloat16),
            pltpu.VMEM((RADIX, 2 * depth, columns), jnp.float32),
            pltpu.VMEM((2, lines, columns), jnp.bfloat16),
            pltpu.VMEM((2, 8, columns), jnp.float32),
            pltpu.VMEM((ranges - 1, 2, 8, columns), jnp.float32),
            pltpu.SemaphoreType.DMA((ranges - 1,)),
            pltpu.SemaphoreType.DMA((ranges - 1,)),
            pltpu.SemaphoreType.DMA((dates - 1,)),
            pltpu.SemaphoreType.DMA((dates - 1,)),
            pltpu.SemaphoreType.DMA,
        ],
        compiler_params=pltpu.CompilerParams(
            collective_id=0, has_side_effects=True, vmem_limit_bytes=VMEM_BYTES
        ),
        name="filter_exchange",
    )(re, im, ref_re, ref_im, weights, jnp.asarray(fwd), jnp.asarray(inv))


def map_kernel(index_ref, pieces_ref, mask_ref, table_ref, out_ref, turned):
    j = pl.program_id(0)
    dates, _, lines_dev, columns = pieces_ref.shape
    groups = lines_dev // ROWS
    depth = 2 * dates * ROWS
    points = out_ref.shape[-1]

    @pl.when(j == 0)
    def _():
        def turn(g, carry):
            rows = pl.ds(pl.multiple_of(g * ROWS, ROWS), ROWS)
            block = pieces_ref[:, :, rows, :].astype(jnp.float32)
            block = block.reshape(2 * dates, ROWS, columns)
            power = jnp.sum(block * block, axis=0) * (1.0 / dates)
            wanted = mask_ref[rows, :].astype(jnp.float32)
            scale = jnp.sqrt(wanted / (dates * jnp.maximum(power, 1.0)))
            scaled = (block * scale[None]).reshape(depth, columns)
            cols = pl.ds(pl.multiple_of(g * columns, columns), columns)
            turned[cols, :] = scaled.T.astype(jnp.bfloat16)
            return carry

        lax.fori_loop(0, groups, turn, 0)

    row = lax.broadcasted_iota(jnp.int32, (depth, 2 * points), 0)
    table = jnp.where(lax.rem(row, ROWS) == j, table_ref[...], 0.0).astype(jnp.bfloat16)
    batch = min(4, groups)

    def multiply(b, carry):
        rows = pl.ds(pl.multiple_of(b * batch * columns, batch * columns), batch * columns)
        peri = jnp.dot(turned[rows, :], table, preferred_element_type=jnp.float32)
        result = peri[:, :points] * peri[:, :points] + peri[:, points:] * peri[:, points:]
        out_ref[pl.ds(b * batch, batch), 0] = result.reshape(batch, columns, points)
        return carry

    lax.fori_loop(0, groups // batch, multiply, 0)


def coherence_map(pieces, mask, table, index):
    dates, _, lines_dev, columns = pieces.shape
    points = table.shape[1] // 2
    groups = lines_dev // ROWS
    depth = 2 * dates * ROWS
    tall = jnp.repeat(table.astype(jnp.bfloat16).astype(jnp.float32), ROWS, axis=0)
    mapped = pl.pallas_call(
        map_kernel,
        out_shape=jax.ShapeDtypeStruct((groups, ROWS, columns, points), jnp.float32),
        grid_spec=pltpu.PrefetchScalarGridSpec(
            num_scalar_prefetch=1,
            grid=(ROWS,),
            in_specs=[
                pl.BlockSpec((dates, 2, lines_dev, columns), lambda j, index: (0, 0, 0, 0)),
                pl.BlockSpec((lines_dev, columns), lambda j, index: (index[0], 0)),
                pl.BlockSpec((depth, 2 * points), lambda j, index: (0, 0)),
            ],
            out_specs=pl.BlockSpec((groups, 1, columns, points), lambda j, index: (0, j, 0, 0)),
            scratch_shapes=[pltpu.VMEM((groups * columns, depth), jnp.bfloat16)],
        ),
        compiler_params=pltpu.CompilerParams(vmem_limit_bytes=VMEM_BYTES),
        name="coherence_map",
    )(index, pieces, mask, tall)
    return mapped.reshape(lines_dev, columns, points)


def shards(slc_re, slc_im, ref_date, gain, bperp, tdays, mask):
    dates = lax.axis_size("date")
    ranges = lax.axis_size("rng")
    own_re, own_im = slc_re[0], slc_im[0]
    ref_re, ref_im = (
        broadcast(own_re, "date", ref_date[0]),
        broadcast(own_im, "date", ref_date[0]),
    )
    pieces = filtered_pieces(dates, ranges, own_re, own_im, ref_re, ref_im, gain)
    index = lax.axis_index("date").astype(jnp.int32).reshape(1)
    return coherence_map(pieces, mask, phase_table(bperp, tdays), index)


def solution(mesh):
    in_specs = (P("date", None, "rng"), P("date", None, "rng"), P(), P(), P(), P(), P(None, "rng"))
    out_specs = P("date", "rng", None)
    return jax.shard_map(shards, mesh=mesh, in_specs=in_specs, out_specs=out_specs, check_vma=False)
```

time: 496 us -> 130 us (0.26); the launches traced: 487 us -> 129 us
  matrix products: 279 us -> 0 us
  other arithmetic: 89 us -> 2.39 us
  Pallas kernels: 0 us -> 53.1 us
  local copies, waits for them, and re-layouts: 25.4 us -> 2.38 us
  starting transfers between devices: 12.7 us -> 0.01 us
  blocking collectives: 10.2 us -> 0 us
    dot_general x5 -> x0, matrix products: 279 us -> none  [the longest x1 64 us: shards(): jnp.einsum('fl,kdlc->kdfc', sin_table, pair, preferred_element_type=jnp.f...]
    pallas_call x0 -> x2, Pallas kernels: none -> 53.1 us  [the longest x1 27.9 us: filtered_pieces(): pl.pallas_call(functools.partial(filter_kernel, dates, ranges), out_shape...]
    div x1 -> x0, other arithmetic: 33.6 us -> none  [coherence_map(): (peri_re * peri_re + peri_im * peri_im) / (date_count * jnp.maximum(pixel...]
    mul x2 -> x0, other arithmetic: 23.6 us -> none  [the longest x1 23.6 us: shards(): return mapped * mask_rows.astype(jnp.float32)[:, :, None]]
    unnamed x2 -> x0, other arithmetic: 23.3 us -> none
    all_to_all x2 -> x0, local copies, waits for them, and re-layouts: 17.5 us -> none  [the longest x1 8.76 us: shards(): lax.all_to_all(filt_re, 'date', split_axis=1, concat_axis=0, tiled=True)]
    all_to_all x2 -> x0, starting transfers between devices: 12.7 us -> none  [the longest x1 8.21 us: shards(): lax.all_to_all(filt_re, 'date', split_axis=1, concat_axis=0, tiled=True)]
    psum x1 -> x0, blocking collectives: 10.2 us -> none  [shards(): date_sums, ref_sum = lax.psum((local_sums, ref_local), 'rng')]
  transfers between devices with their start and end apart: 3 -> 1, of which waited for: 1 -> 1; matrix products, arithmetic and copies ran while one was open for 5% -> 0% of each run, Pallas kernels for 0% -> 0%
where the time goes in v1:
time: 130 us; the launch traced here: 129 us
  waiting for transfers between devices  56.7 us (44%)
  Pallas kernels  53.1 us (41%)
  between operations  14.2 us (11%)
  other arithmetic  2.39 us (2%)
  local copies, waits for them, and re-layouts  2.38 us (2%)
    psum x1, waiting for transfers between devices, broadcast(): return lax.psum(jnp.where(mine, shard, jnp.zeros_like(shard)), axis)  56.7 us
    pallas_call x1, Pallas kernels, filtered_pieces(): pl.pallas_call(functools.partial(filter_kernel, dates, ranges), out_shape...  27.9 us
    pallas_call x1, Pallas kernels, coherence_map(): pl.pallas_call(map_kernel, out_shape=jax.ShapeDtypeStruct((groups, ROWS,...  25.2 us
  transfers between devices with their start and end apart: 1, of which 1 were waited for; matrix products, arithmetic and copies ran while one was open for 0% of the time, Pallas kernels for 0%

profile of v1, /device:TPU:3, one launch (start us, length us, event | category | flops | bytes accessed | tf_op | source)
XLA Modules:
  0.0 128.8 jit_solution(8623894318358839648)
XLA Ops:
  6.5 0.0 copy-start.1
  6.5 0.0 copy-start.2
  6.5 0.0 copy-start
  6.5 0.0 all-reduce.3.cloned.1.call-start
  7.2 2.2 %broadcast_select_fusion = (bf16[2048,128]{1,0:T(8,128)(2,1)}, bf16[2048,128]{1,0:T(8,128)(2,1)}) fusion(pred[]{:T(512)S(6)} %eq.8, bf16[1,2048,128]{2,1,0:T(8,128)(2,1)} %param.10, bf16[1,2048,128]{2,1,0:T(8,128)(2,1)} %param.9), kind=kLoop, calls=%fused_computation | loop fusion | flops 524288 | bytes 2097153 | tf_op jit(solution)/shard_map/jit(_where)/select_n | solution.py:24
  9.5 0.0 all-reduce.3.cloned.1.call-update
  9.5 0.0 copy-done.1
  9.5 0.0 copy-done.2
  9.5 0.1 negate_convert_fusion
  9.8 0.0 copy-done
  9.8 0.1 reshape.42
  9.9 0.1 copy.12
  9.9 56.7 %all-reduce.3.cloned.1.call-done = (bf16[2048,128]{1,0:T(8,128)(2,1)}, bf16[2048,128]{1,0:T(8,128)(2,1)}) async-done(((bf16[2048,128]{1,0:T(8,128)(2,1)}, bf16[2048,128]{1,0:T(8,128)(2,1)}), (bf16[2048,128]{1,0:T(8,128)(2,1)}, bf16[2048,128]{1,0:T(8,128)(2,1)})) %all-reduce.3.cloned.1.call-update) | async-done | bytes 1048592 | tf_op jit(solution)/shard_map/psum | solution.py:24
  66.6 1.3 %broadcast_in_dim.4.gain_ref = f32[16,128,128]{2,1,0:T(8,128)} broadcast(f32[16,128]{1,0:T(8,128)S(1)} %copy.12), dimensions={0,1} | broadcast | bytes 1056768 | tf_op jit(solution)/shard_map/broadcast_in_dim | solution.py:232
  67.9 27.9 %filter_exchange.1.pieces_ref = bf16[8,2,256,128]{3,2,1,0:T(8,128)(2,1)} custom-call(bf16[2048,128]{1,0:T(8,128)(2,1)} %bitcast.15, bf16[2048,128]{1,0:T(8,128)(2,1)} %bitcast.16, bf16[2048,128]{1,0:T(8,128)(2,1)} %get-tuple-element.5.ref_re_ref, bf16[2048,128]{1,0:T(8,128)(2,1)} %get-tuple-element.6.ref_im_ref, f32[16,128,128]{2,1,0:T(8,128)} %broadcast_in_dim.4.gain_ref, ...), custom_call_target="tpu_custom_call" | custom-call | tf_op jit(solution)/shard_map/filter_exchange/pallas_call | solution.py:234
  95.8 0.9 broadcast_in_dim.5
  96.7 25.2 %coherence_map.1 = f32[16,16,128,256]{3,2,1,0:T(8,128)} custom-call(s32[1]{0:T(128)} %bitcast.index_ref, bf16[8,2,256,128]{3,2,1,0:T(8,128)(2,1)} %filter_exchange.1.pieces_ref, s32[2048,128]{1,0:T(8,128)} %mask_ref.1, f32[256,512]{1,0:T(8,128)} %bitcast.14), custom_call_target="tpu_custom_call" | custom-call | tf_op jit(solution)/shard_map/coherence_map/pallas_call | solution.py:301
  (5 shorter events, 0.1 us)
Async XLA Ops:
  6.5 3.0 %copy-start.1 = (s32[8]{0:T(128)S(1)}, s32[8]{0:T(128)}, u32[]{:S(2)}) copy-start(s32[8]{0:T(128)} %param.14) | copy-start | bytes 100
  6.5 3.0 %copy-start.2 = (s32[8]{0:T(128)S(1)}, s32[8]{0:T(128)}, u32[]{:S(2)}) copy-start(s32[8]{0:T(128)} %param.13) | copy-start | bytes 100
  6.5 3.2 %copy-start = (f32[2048]{0:T(1024)S(1)}, f32[2048]{0:T(1024)}, u32[]{:S(2)}) copy-start(f32[2048]{0:T(1024)} %param.12) | copy-start | bytes 24580
  6.5 60.0 %all-reduce.3.cloned.1.call-start = ((), (), s32[]{:S(2)}) async-start(), calls=%async_computation | async-start | bytes 2097152 | tf_op jit(solution)/shard_map/psum | solution.py:24
Sparse Core Ops, SparseCore 0:
  10.6 55.9 all-reduce.2

commit v2 on v1

--- a/solution.py
+++ b/solution.py
@@ -14,6 +14,7 @@
 VGRID = 16
 PHASE_Q = 1024
 RADIX = 16
+CHUNKS = 8
 ROWS = 16
 MESH = pl.DeviceIdType.MESH
 VMEM_BYTES = 56 * 1024 * 1024
@@ -102,10 +103,182 @@
     return out
 
 
+def local_power(re_ref, im_ref):
+    def add(i, total):
+        rows = pl.ds(pl.multiple_of(i * 128, 128), 128)
+        a = re_ref[rows, :].astype(jnp.float32)
+        b = im_ref[rows, :].astype(jnp.float32)
+        return total + jnp.sum((a * a + b * b).reshape(16, 8, 128), axis=0)
+
+    return lax.fori_loop(0, re_ref.shape[0] // 128, add, jnp.zeros((8, 128), jnp.float32))
+
+
+def share_kernel(
+    owner, dates, ranges, re_ref, im_ref, image_ref, total_ref, sums, peer_sums,
+    sum_send, sum_recv, total_send, total_recv, send_sem, recv_sem, own_sem,
+):
+    date = lax.axis_index("date")
+    rng = lax.axis_index("rng")
+    inputs = (re_ref, im_ref)
+    chunk = re_ref.shape[0] // CHUNKS
+    barrier = pltpu.get_barrier_semaphore()
+    for step in range(1, dates):
+        other = lax.rem(date + step, dates)
+        pl.semaphore_signal(barrier, inc=1, device_id=(other, rng), device_id_type=MESH)
+    for step in range(1, ranges):
+        other = lax.rem(rng + step, ranges)
+        pl.semaphore_signal(barrier, inc=1, device_id=(date, other), device_id_type=MESH)
+    sums[...] = local_power(re_ref, im_ref)
+    pl.semaphore_wait(barrier, dates - 1 + ranges - 1)
+
+    def sum_copy(step):
+        return pltpu.make_async_remote_copy(
+            src_ref=sums, dst_ref=peer_sums.at[step - 1],
+            send_sem=sum_send.at[step - 1], recv_sem=sum_recv.at[step - 1],
+            device_id=(date, lax.rem(rng + step, ranges)), device_id_type=MESH,
+        )
+
+    def finish_sums():
+        total = sums[...]
+        for step in range(1, ranges):
+            sum_copy(step).wait()
+            total = total + peer_sums[step - 1]
+        total_ref[0] = total
+
+    def total_copy(step):
+        return pltpu.make_async_remote_copy(
+            src_ref=total_ref.at[0], dst_ref=total_ref.at[1],
+            send_sem=total_send.at[step - 1], recv_sem=total_recv,
+            device_id=((owner + step) % dates, rng), device_id_type=MESH,
+        )
+
+    def image_copy(k, n, way, target):
+        rows = pl.ds(n * chunk, chunk)
+        return lambda source: pltpu.make_async_remote_copy(
+            src_ref=source.at[rows, :], dst_ref=image_ref.at[k, rows, :],
+            send_sem=send_sem.at[k, n, way], recv_sem=recv_sem.at[k, n],
+            device_id=(target, rng), device_id_type=MESH,
+        )
+
+    for step in range(1, ranges):
+        sum_copy(step).start()
+
+    o, o2 = owner, owner ^ 1
+    x, x2 = owner ^ 2, owner ^ 3
+    y, y2 = owner ^ 4, owner ^ 5
+    z, z2 = owner ^ 6, owner ^ 7
+
+    @pl.when(date == o)
+    def _():
+        def copies(n):
+            made = []
+            for k in range(2):
+                for way, target in enumerate(((x, y)[k], o2)):
+                    made.append(image_copy(k, n, way, target)(inputs[k]))
+            return made
+
+        ahead = 3
+        for n in range(ahead):
+            for copy in copies(n):
+                copy.start()
+        finish_sums()
+        for step in range(1, dates):
+            total_copy(step).start()
+        total_ref[1] = total_ref[0]
+        for n in range(ahead, CHUNKS + ahead):
+            for copy in copies(n - ahead):
+                copy.wait_send()
+            if n < CHUNKS:
+                for copy in copies(n):
+                    copy.start()
+        for k in range(2):
+            own = pltpu.make_async_copy(inputs[k], image_ref.at[k], own_sem.at[k])
+            own.start()
+            own.wait()
+        for step in range(1, dates):
+            total_copy(step).wait_send()
+
+    routes = (
+        (x, x2, (z, None), (1, 3)),
+        (y, y2, (None, z), (3, 1)),
+        (z, z2, (y, x), (2, 2)),
+    )
+    for device, partner, onward, delays in routes:
+        @pl.when(date == device)
+        def _(device=device, partner=partner, onward=onward, delays=delays):
+            started = []
+            for t in range(CHUNKS + 3):
+                for k in range(2):
+                    n = t - delays[k]
+                    if not 0 <= n < CHUNKS:
+                        continue
+                    image_copy(k, n, 1, partner)(image_ref.at[k]).wait_recv()
+                    for way, target in enumerate((onward[k], partner)):
+                        if target is not None:
+                            copy = image_copy(k, n, way, target)(image_ref.at[k])
+                            copy.start()
+                            started.append(copy)
+            finish_sums()
+            for copy in started:
+                copy.wait_send()
+            total_copy(1).wait_recv()
+
+    for device in (o2, x2, y2, z2):
+        @pl.when(date == device)
+        def _(device=device):
+            finish_sums()
+            for n in range(CHUNKS):
+                for k in range(2):
+                    image_copy(k, n, 1, device ^ 1)(image_ref.at[k]).wait_recv()
+            total_copy(1).wait_recv()
+
+
+def share_from(owner, dates, ranges, re, im):
+    lines, columns = re.shape
+    vmem = pl.BlockSpec(memory_space=pltpu.VMEM)
+    return pl.pallas_call(
+        functools.partial(share_kernel, owner, dates, ranges),
+        out_shape=(
+            jax.ShapeDtypeStruct((2, lines, columns), jnp.bfloat16),
+            jax.ShapeDtypeStruct((2, 8, columns), jnp.float32),
+        ),
+        in_specs=[vmem] * 2,
+        out_specs=(vmem, vmem),
+        scratch_shapes=[
+            pltpu.VMEM((8, columns), jnp.float32),
+            pltpu.VMEM((ranges - 1, 8, columns), jnp.float32),
+            pltpu.SemaphoreType.DMA((ranges - 1,)),
+            pltpu.SemaphoreType.DMA((ranges - 1,)),
+            pltpu.SemaphoreType.DMA((dates - 1,)),
+            pltpu.SemaphoreType.DMA,
+            pltpu.SemaphoreType.DMA((2, CHUNKS, 2)),
+            pltpu.SemaphoreType.DMA((2, CHUNKS)),
+            pltpu.SemaphoreType.DMA((2,)),
+        ],
+        compiler_params=pltpu.CompilerParams(
+            collective_id=1 + owner, has_side_effects=True, vmem_limit_bytes=VMEM_BYTES
+        ),
+        name=f"share_{owner}",
+    )(re, im)
+
+
+def power_rows(re, im):
+    wide_re, wide_im = re.astype(jnp.float32), im.astype(jnp.float32)
+    return jnp.sum((wide_re * wide_re + wide_im * wide_im).reshape(-1, 8, re.shape[1]), axis=0)
+
+
+def share_reference(dates, ranges, re, im, ref_date):
+    if dates == 8:
+        branches = [functools.partial(share_from, owner, dates, ranges) for owner in range(dates)]
+        return lax.switch(ref_date, branches, re, im)
+    image = jnp.stack([broadcast(re, "date", ref_date), broadcast(im, "date", ref_date)])
+    sums = jnp.stack([power_rows(re, im), power_rows(image[0], image[1])])
+    return image, lax.psum(sums, "rng")
+
+
 def filter_kernel(
-    dates, ranges, re_ref, im_ref, ref_re_ref, ref_im_ref, gain_ref, fwd_ref, inv_ref,
-    out_ref, spec, back, filt, sums, peer_sums,
-    sum_send, sum_recv, send_sem, recv_sem, own_sem,
+    dates, ranges, re_ref, im_ref, image_ref, total_ref, gain_ref, fwd_ref, inv_ref,
+    out_ref, spec, back, filt, send_sem, recv_sem, own_sem,
 ):
     date = lax.axis_index("date")
     rng = lax.axis_index("rng")
@@ -122,36 +295,7 @@
         return carry
 
     lax.fori_loop(1, dates, greet, 0)
-    for step in range(1, ranges):
-        other = lax.rem(rng + step, ranges)
-        pl.semaphore_signal(barrier, inc=1, device_id=(date, other), device_id_type=MESH)
-
-    for k, (a_ref, b_ref) in enumerate(((re_ref, im_ref), (ref_re_ref, ref_im_ref))):
-        def add(i, total, a_ref=a_ref, b_ref=b_ref):
-            rows = pl.ds(pl.multiple_of(i * 128, 128), 128)
-            a = a_ref[rows, :].astype(jnp.float32)
-            b = b_ref[rows, :].astype(jnp.float32)
-            return total + jnp.sum((a * a + b * b).reshape(16, 8, 128), axis=0)
-
-        sums[k] = lax.fori_loop(0, lines // 128, add, jnp.zeros((8, 128), jnp.float32))
-
-    pl.semaphore_wait(barrier, dates - 1 + ranges - 1)
-    sum_copies = []
-    for step in range(1, ranges):
-        other = lax.rem(rng + step, ranges)
-        copy = pltpu.make_async_remote_copy(
-            src_ref=sums, dst_ref=peer_sums.at[step - 1],
-            send_sem=sum_send.at[step - 1], recv_sem=sum_recv.at[step - 1],
-            device_id=(date, other), device_id_type=MESH,
-        )
-        copy.start()
-        sum_copies.append(copy)
-    for copy in sum_copies:
-        copy.wait()
-    total = sums[...]
-    for step in range(1, ranges):
-        total = total + peer_sums[step - 1]
-    power = jnp.sum(total, axis=(1, 2), keepdims=True) * (1.0 / pixels)
+    power = jnp.sum(total_ref[...], axis=(1, 2), keepdims=True) * (1.0 / pixels)
     scale = lax.rsqrt(power + 1e-06)
     own_scale, ref_scale = scale[0], scale[1]
 
@@ -161,8 +305,8 @@
             rows = pl.ds(pl.multiple_of(l1 * depth + q * ROWS, ROWS), ROWS)
             own_re = re_ref[rows, :].astype(jnp.float32) * own_scale
             own_im = im_ref[rows, :].astype(jnp.float32) * own_scale
-            ref_re = ref_re_ref[rows, :].astype(jnp.float32) * ref_scale
-            ref_im = ref_im_ref[rows, :].astype(jnp.float32) * ref_scale
+            ref_re = image_ref[0, rows, :].astype(jnp.float32) * ref_scale
+            ref_im = image_ref[1, rows, :].astype(jnp.float32) * ref_scale
             ifg_re = (own_re * ref_re + own_im * ref_im).astype(jnp.bfloat16)
             ifg_im = (own_im * ref_re - own_re * ref_im).astype(jnp.bfloat16)
             values.append((ifg_re.astype(jnp.float32), ifg_im.astype(jnp.float32)))
@@ -217,6 +361,7 @@
         piece(step).wait()
         return carry
 
+    pl.semaphore_wait(barrier, dates - 1)
     own = pltpu.make_async_copy(block(date), out_ref.at[date], own_sem)
     lax.fori_loop(1, dates, send, 0)
     own.start()
@@ -224,7 +369,7 @@
     lax.fori_loop(1, dates, finish, 0)
 
 
-def filtered_pieces(dates, ranges, re, im, ref_re, ref_im, gain):
+def filtered_pieces(dates, ranges, re, im, image, totals, gain):
     lines, columns = re.shape
     depth = lines // RADIX
     lines_dev = lines // dates
@@ -240,10 +385,6 @@
             pltpu.VMEM((RADIX, 2 * depth, columns), jnp.bfloat16),
             pltpu.VMEM((RADIX, 2 * depth, columns), jnp.float32),
             pltpu.VMEM((2, lines, columns), jnp.bfloat16),
-            pltpu.VMEM((2, 8, columns), jnp.float32),
-            pltpu.VMEM((ranges - 1, 2, 8, columns), jnp.float32),
-            pltpu.SemaphoreType.DMA((ranges - 1,)),
-            pltpu.SemaphoreType.DMA((ranges - 1,)),
             pltpu.SemaphoreType.DMA((dates - 1,)),
             pltpu.SemaphoreType.DMA((dates - 1,)),
             pltpu.SemaphoreType.DMA,
@@ -252,7 +393,7 @@
             collective_id=0, has_side_effects=True, vmem_limit_bytes=VMEM_BYTES
         ),
         name="filter_exchange",
-    )(re, im, ref_re, ref_im, weights, jnp.asarray(fwd), jnp.asarray(inv))
+    )(re, im, image, totals, weights, jnp.asarray(fwd), jnp.asarray(inv))
 
 
 def map_kernel(index_ref, pieces_ref, mask_ref, table_ref, out_ref, turned):
@@ -279,7 +420,7 @@
         lax.fori_loop(0, groups, turn, 0)
 
     row = lax.broadcasted_iota(jnp.int32, (depth, 2 * points), 0)
-    table = jnp.where(lax.rem(row, ROWS) == j, table_ref[...], 0.0).astype(jnp.bfloat16)
+    table = jnp.where((row & (ROWS - 1)) == j, table_ref[...], 0.0).astype(jnp.bfloat16)
     batch = min(4, groups)
 
     def multiply(b, carry):
@@ -289,7 +430,7 @@
         out_ref[pl.ds(b * batch, batch), 0] = result.reshape(batch, columns, points)
         return carry
 
-    lax.fori_loop(0, groups // batch, multiply, 0)
+    lax.fori_loop(0, groups // batch, multiply, 0, unroll=True)
 
 
 def coherence_map(pieces, mask, table, index):
@@ -322,11 +463,8 @@
     dates = lax.axis_size("date")
     ranges = lax.axis_size("rng")
     own_re, own_im = slc_re[0], slc_im[0]
-    ref_re, ref_im = (
-        broadcast(own_re, "date", ref_date[0]),
-        broadcast(own_im, "date", ref_date[0]),
-    )
-    pieces = filtered_pieces(dates, ranges, own_re, own_im, ref_re, ref_im, gain)
+    image, totals = share_reference(dates, ranges, own_re, own_im, ref_date[0])
+    pieces = filtered_pieces(dates, ranges, own_re, own_im, image, totals, gain)
     index = lax.axis_index("date").astype(jnp.int32).reshape(1)
     return coherence_map(pieces, mask, phase_table(bperp, tdays), index)
 

time: 130 us -> 82.9 us (0.64)
  waiting for transfers between devices: 56.7 us -> 0 us
  Pallas kernels: 53.1 us -> 78 us
  between operations: 14.2 us -> 0.72 us
  other arithmetic: 2.39 us -> 0.82 us
    psum x1 -> x0, waiting for transfers between devices: 56.7 us -> none  [broadcast(): return lax.psum(jnp.where(mine, shard, jnp.zeros_like(shard)), axis)]
    pallas_call x0 -> x1, Pallas kernels: none -> 31.5 us  [share_from(): pl.pallas_call(functools.partial(share_kernel, owner, dates, ranges), out...]
    pallas_call x1, Pallas kernels: 25.2 us -> 20.7 us  [coherence_map(): pl.pallas_call(map_kernel, out_shape=jax.ShapeDtypeStruct((groups, ROWS,...]
    select_n x1 -> x0, other arithmetic: 2.24 us -> none  [broadcast(): return lax.psum(jnp.where(mine, shard, jnp.zeros_like(shard)), axis)]
    pallas_call x1, Pallas kernels: 27.9 us -> 25.9 us  [filtered_pieces(): pl.pallas_call(functools.partial(filter_kernel, dates, ranges), out_shape...]
  transfers between devices with their start and end apart: 1 -> 0, of which waited for: 1 -> 0; matrix products, arithmetic and copies ran while one was open for 0% -> 0% of each run, Pallas kernels for 0% -> 0%
where the time goes in v2:
time: 82.9 us; the launch traced here: 82.7 us
  Pallas kernels  78 us (94%)
  local copies, waits for them, and re-layouts  3.08 us (4%)
    pallas_call x1, Pallas kernels, share_from(): pl.pallas_call(functools.partial(share_kernel, owner, dates, ranges), out...  31.5 us
    pallas_call x1, Pallas kernels, filtered_pieces(): pl.pallas_call(functools.partial(filter_kernel, dates, ranges), out_shape...  25.9 us
    pallas_call x1, Pallas kernels, coherence_map(): pl.pallas_call(map_kernel, out_shape=jax.ShapeDtypeStruct((groups, ROWS,...  20.7 us

profile of v2, /device:TPU:3, one launch (start us, length us, event | category | flops | bytes accessed | tf_op | source)
XLA Modules:
  0.0 82.7 jit_solution(17158512109998349137)
XLA Ops:
  0.7 0.8 negate_convert_fusion
  1.6 0.8 reshape.45
  2.3 0.1 copy.12
  2.4 0.9 %broadcast_in_dim.5 = f32[16,16,512]{2,1,0:T(8,128)} broadcast(f32[16,512]{1,0:T(8,128)S(1)} %reshape.48), dimensions={0,2} | broadcast | bytes 557056 | tf_op jit(solution)/shard_map/broadcast_in_dim | solution.py:441
  3.3 1.3 %broadcast_in_dim.4.gain_ref = f32[16,128,128]{2,1,0:T(8,128)} broadcast(f32[16,128]{1,0:T(8,128)S(1)} %copy.12), dimensions={0,1} | broadcast | bytes 1056768 | tf_op jit(solution)/shard_map/broadcast_in_dim | solution.py:377
  4.6 31.5 %conditional.1 = ((bf16[2,2048,128]{2,1,0:T(8,128)(2,1)S(1)}, f32[2,8,128]{2,1,0:T(8,128)S(1)})) conditional(s32[]{:T(128)} %bitcast.3, (bf16[2048,128]{1,0:T(8,128)(2,1)}, bf16[2048,128]{1,0:T(8,128)(2,1)}) %tuple.58, (bf16[2048,128]{1,0:T(8,128)(2,1)}, bf16[2048,128]{1,0:T(8,128)(2,1)}) %tuple.59, ...), branch_computations={%region_0.0_spmd, %region_1.0_spmd, %region_2.0_spmd, %region_3.0_... | conditional | bytes 8 | solution.py:273
  4.6 31.5 %share_6.1 = (bf16[2,2048,128]{2,1,0:T(8,128)(2,1)S(1)}, f32[2,8,128]{2,1,0:T(8,128)S(1)}) custom-call(bf16[2048,128]{1,0:T(8,128)(2,1)} %get-tuple-element.49.re_ref, bf16[2048,128]{1,0:T(8,128)(2,1)} %get-tuple-element.50.im_ref), custom_call_target="tpu_custom_call" | custom-call | tf_op jit(solution)/shard_map/cond/branch_6_fun/share_6/pallas_call | solution.py:239
  36.1 25.9 %filter_exchange.1.pieces_ref = bf16[8,2,256,128]{3,2,1,0:T(8,128)(2,1)} custom-call(bf16[2048,128]{1,0:T(8,128)(2,1)} %bitcast.19, bf16[2048,128]{1,0:T(8,128)(2,1)} %bitcast.28, bf16[2,2048,128]{2,1,0:T(8,128)(2,1)S(1)} %get-tuple-element.55.image_ref, f32[2,8,128]{2,1,0:T(8,128)S(1)} %get-tuple-element.56.total_ref, ...), custom_call_target="tpu_custom_call" | custom-call | tf_op jit(solution)/shard_map/filter_exchange/pallas_call | solution.py:379
  62.0 20.7 %coherence_map.1 = f32[16,16,128,256]{3,2,1,0:T(8,128)} custom-call(s32[1]{0:T(128)} %bitcast.index_ref, bf16[8,2,256,128]{3,2,1,0:T(8,128)(2,1)} %filter_exchange.1.pieces_ref, s32[2048,128]{1,0:T(8,128)} %mask_ref.1, f32[256,512]{1,0:T(8,128)} %bitcast.29), custom_call_target="tpu_custom_call" | custom-call | tf_op jit(solution)/shard_map/coherence_map/pallas_call | solution.py:442
  (5 shorter events, 0.1 us)

commit v3 on v2

--- a/solution.py
+++ b/solution.py
@@ -49,9 +49,13 @@
     angles = quanta.astype(jnp.float32) * (2.0 * math.pi / PHASE_Q)
     phase_re = jnp.cos(angles)
     phase_im = jnp.sin(angles)
-    upper = jnp.concatenate([phase_re, -phase_im], axis=1)
-    lower = jnp.concatenate([phase_im, phase_re], axis=1)
-    return jnp.stack([upper, lower], axis=1).reshape(-1, 2 * HGRID * VGRID)
+    half = HGRID * VGRID // 2
+    upper, lower = [], []
+    for part in (slice(0, half), slice(half, 2 * half)):
+        upper += [phase_re[:, part], -phase_im[:, part]]
+        lower += [phase_im[:, part], phase_re[:, part]]
+    rows = [jnp.concatenate(upper, axis=1), jnp.concatenate(lower, axis=1)]
+    return jnp.concatenate(rows, axis=0).astype(jnp.bfloat16).astype(jnp.float32)
 
 
 def radix4(a, b, c, d, sign):
@@ -177,10 +181,15 @@
                     made.append(image_copy(k, n, way, target)(inputs[k]))
             return made
 
-        ahead = 3
+        owns = [
+            pltpu.make_async_copy(inputs[k], image_ref.at[k], own_sem.at[k]) for k in range(2)
+        ]
+        ahead = 4
         for n in range(ahead):
             for copy in copies(n):
                 copy.start()
+        for own in owns:
+            own.start()
         finish_sums()
         for step in range(1, dates):
             total_copy(step).start()
@@ -191,23 +200,21 @@
             if n < CHUNKS:
                 for copy in copies(n):
                     copy.start()
-        for k in range(2):
-            own = pltpu.make_async_copy(inputs[k], image_ref.at[k], own_sem.at[k])
-            own.start()
+        for own in owns:
             own.wait()
         for step in range(1, dates):
             total_copy(step).wait_send()
 
     routes = (
-        (x, x2, (z, None), (1, 3)),
-        (y, y2, (None, z), (3, 1)),
-        (z, z2, (y, x), (2, 2)),
+        (x, x2, (z, None), (0, 6)),
+        (y, y2, (None, z), (6, 0)),
+        (z, z2, (y, x), (0, 0)),
     )
     for device, partner, onward, delays in routes:
         @pl.when(date == device)
         def _(device=device, partner=partner, onward=onward, delays=delays):
             started = []
-            for t in range(CHUNKS + 3):
+            for t in range(CHUNKS + 6):
                 for k in range(2):
                     n = t - delays[k]
                     if not 0 <= n < CHUNKS:
@@ -278,7 +285,7 @@
 
 def filter_kernel(
     dates, ranges, re_ref, im_ref, image_ref, total_ref, gain_ref, fwd_ref, inv_ref,
-    out_ref, spec, back, filt, send_sem, recv_sem, own_sem,
+    out_ref, spec, back, filt, fwd, inv, send_sem, recv_sem, own_sem, table_sem,
 ):
     date = lax.axis_index("date")
     rng = lax.axis_index("rng")
@@ -287,6 +294,12 @@
     lines_dev = lines // dates
     pixels = lines * re_ref.shape[1] * ranges
 
+    loads = [
+        pltpu.make_async_copy(fwd_ref, fwd, table_sem.at[0]),
+        pltpu.make_async_copy(inv_ref, inv, table_sem.at[1]),
+    ]
+    for load in loads:
+        load.start()
     barrier = pltpu.get_barrier_semaphore()
 
     def greet(step, carry):
@@ -319,12 +332,15 @@
 
     lax.fori_loop(0, depth // ROWS, forward, 0)
 
+    for load in loads:
+        load.wait()
+
     def band(f1, carry):
-        spectrum = jnp.dot(fwd_ref[f1], spec[f1], preferred_element_type=jnp.float32)
-        weight = gain_ref[f1]
+        spectrum = jnp.dot(fwd[f1], spec[f1], preferred_element_type=jnp.float32)
+        weight = jnp.broadcast_to(gain_ref[pl.ds(f1, 1), :], (spectrum.shape[1], depth)).T
         weighted = jnp.concatenate([spectrum[:depth] * weight, spectrum[depth:] * weight], axis=0)
         back[f1] = jnp.dot(
-            inv_ref[f1], weighted.astype(jnp.bfloat16), preferred_element_type=jnp.float32
+            inv[f1], weighted.astype(jnp.bfloat16), preferred_element_type=jnp.float32
         )
         return carry
 
@@ -348,7 +364,7 @@
     def piece(step):
         other = lax.rem(date + step, dates)
         return pltpu.make_async_remote_copy(
-            src_ref=block(other), dst_ref=out_ref.at[date],
+            src_ref=block(other), dst_ref=out_ref.at[:, date],
             send_sem=send_sem.at[step - 1], recv_sem=recv_sem.at[step - 1],
             device_id=(other, rng), device_id_type=MESH,
         )
@@ -362,7 +378,7 @@
         return carry
 
     pl.semaphore_wait(barrier, dates - 1)
-    own = pltpu.make_async_copy(block(date), out_ref.at[date], own_sem)
+    own = pltpu.make_async_copy(block(date), out_ref.at[:, date], own_sem)
     lax.fori_loop(1, dates, send, 0)
     own.start()
     own.wait()
@@ -374,20 +390,23 @@
     depth = lines // RADIX
     lines_dev = lines // dates
     fwd, inv = dft_blocks(lines)
-    weights = jnp.broadcast_to(gain.reshape(depth, RADIX).T[:, :, None], (RADIX, depth, columns))
+    weights = gain.reshape(depth, RADIX).T
     vmem = pl.BlockSpec(memory_space=pltpu.VMEM)
     return pl.pallas_call(
         functools.partial(filter_kernel, dates, ranges),
-        out_shape=jax.ShapeDtypeStruct((dates, 2, lines_dev, columns), jnp.bfloat16),
-        in_specs=[vmem] * 7,
+        out_shape=jax.ShapeDtypeStruct((2, dates, lines_dev, columns), jnp.bfloat16),
+        in_specs=[vmem] * 5 + [pl.BlockSpec(memory_space=pl.ANY)] * 2,
         out_specs=pl.BlockSpec(memory_space=pl.ANY),
         scratch_shapes=[
             pltpu.VMEM((RADIX, 2 * depth, columns), jnp.bfloat16),
             pltpu.VMEM((RADIX, 2 * depth, columns), jnp.float32),
             pltpu.VMEM((2, lines, columns), jnp.bfloat16),
+            pltpu.VMEM(fwd.shape, jnp.bfloat16),
+            pltpu.VMEM(inv.shape, jnp.bfloat16),
             pltpu.SemaphoreType.DMA((dates - 1,)),
             pltpu.SemaphoreType.DMA((dates - 1,)),
             pltpu.SemaphoreType.DMA,
+            pltpu.SemaphoreType.DMA((2,)),
         ],
         compiler_params=pltpu.CompilerParams(
             collective_id=0, has_side_effects=True, vmem_limit_bytes=VMEM_BYTES
@@ -396,9 +415,9 @@
     )(re, im, image, totals, weights, jnp.asarray(fwd), jnp.asarray(inv))
 
 
-def map_kernel(index_ref, pieces_ref, mask_ref, table_ref, out_ref, turned):
+def map_kernel(index_ref, pieces_ref, mask_ref, table_ref, out_ref, turned, tall):
     j = pl.program_id(0)
-    dates, _, lines_dev, columns = pieces_ref.shape
+    _, dates, lines_dev, columns = pieces_ref.shape
     groups = lines_dev // ROWS
     depth = 2 * dates * ROWS
     points = out_ref.shape[-1]
@@ -417,28 +436,39 @@
             turned[cols, :] = scaled.T.astype(jnp.bfloat16)
             return carry
 
-        lax.fori_loop(0, groups, turn, 0)
+        lax.fori_loop(0, groups, turn, 0, unroll=2)
+        for k in range(2 * dates):
+            tall[pl.ds(k * ROWS, ROWS), :] = jnp.broadcast_to(
+                table_ref[pl.ds(k, 1), :], (ROWS, 2 * points)
+            )
 
     row = lax.broadcasted_iota(jnp.int32, (depth, 2 * points), 0)
-    table = jnp.where((row & (ROWS - 1)) == j, table_ref[...], 0.0).astype(jnp.bfloat16)
+    table = jnp.where((row & (ROWS - 1)) == j, tall[...], 0.0).astype(jnp.bfloat16)
     batch = min(4, groups)
 
     def multiply(b, carry):
         rows = pl.ds(pl.multiple_of(b * batch * columns, batch * columns), batch * columns)
-        peri = jnp.dot(turned[rows, :], table, preferred_element_type=jnp.float32)
-        result = peri[:, :points] * peri[:, :points] + peri[:, points:] * peri[:, points:]
-        out_ref[pl.ds(b * batch, batch), 0] = result.reshape(batch, columns, points)
+        source = turned[rows, :]
+        half = points // 2
+        for part in range(2):
+            peri = jnp.dot(
+                source, table[:, part * points:(part + 1) * points],
+                preferred_element_type=jnp.float32,
+            )
+            result = peri[:, :half] * peri[:, :half] + peri[:, half:] * peri[:, half:]
+            out_ref[pl.ds(b * batch, batch), 0, :, pl.ds(part * half, half)] = result.reshape(
+                batch, columns, half
+            )
         return carry
 
     lax.fori_loop(0, groups // batch, multiply, 0, unroll=True)
 
 
 def coherence_map(pieces, mask, table, index):
-    dates, _, lines_dev, columns = pieces.shape
+    _, dates, lines_dev, columns = pieces.shape
     points = table.shape[1] // 2
     groups = lines_dev // ROWS
     depth = 2 * dates * ROWS
-    tall = jnp.repeat(table.astype(jnp.bfloat16).astype(jnp.float32), ROWS, axis=0)
     mapped = pl.pallas_call(
         map_kernel,
         out_shape=jax.ShapeDtypeStruct((groups, ROWS, columns, points), jnp.float32),
@@ -446,16 +476,19 @@
             num_scalar_prefetch=1,
             grid=(ROWS,),
             in_specs=[
-                pl.BlockSpec((dates, 2, lines_dev, columns), lambda j, index: (0, 0, 0, 0)),
+                pl.BlockSpec((2, dates, lines_dev, columns), lambda j, index: (0, 0, 0, 0)),
                 pl.BlockSpec((lines_dev, columns), lambda j, index: (index[0], 0)),
-                pl.BlockSpec((depth, 2 * points), lambda j, index: (0, 0)),
+                pl.BlockSpec((2 * dates, 2 * points), lambda j, index: (0, 0)),
             ],
             out_specs=pl.BlockSpec((groups, 1, columns, points), lambda j, index: (0, j, 0, 0)),
-            scratch_shapes=[pltpu.VMEM((groups * columns, depth), jnp.bfloat16)],
+            scratch_shapes=[
+                pltpu.VMEM((groups * columns, depth), jnp.bfloat16),
+                pltpu.VMEM((depth, 2 * points), jnp.float32),
+            ],
         ),
         compiler_params=pltpu.CompilerParams(vmem_limit_bytes=VMEM_BYTES),
         name="coherence_map",
-    )(index, pieces, mask, tall)
+    )(index, pieces, mask, table)
     return mapped.reshape(lines_dev, columns, points)
 
 

time: 82.9 us -> 66 us (0.80); the launches traced: 82.7 us -> 66.7 us
  Pallas kernels: 78 us -> 62.3 us
  local copies, waits for them, and re-layouts: 3.08 us -> 1.45 us
  other arithmetic: 0.82 us -> 2.23 us
    pallas_call x1, Pallas kernels: 31.5 us -> 10.8 us  [share_from(): pl.pallas_call(functools.partial(share_kernel, owner, dates, ranges), out...]
    pallas_call x1, Pallas kernels: 25.9 us -> 31.9 us  [filtered_pieces(): pl.pallas_call(functools.partial(filter_kernel, dates, ranges), out_shape...]
    broadcast_in_dim x2 -> x0, local copies, waits for them, and re-layouts: 2.2 us -> none  [the longest x1 1.3 us: filtered_pieces(): jnp.broadcast_to(gain.reshape(depth, RADIX).T[:, :, None], (RADIX, depth,...]
    pallas_call x1, Pallas kernels: 20.7 us -> 19.6 us  [coherence_map(): pl.pallas_call(map_kernel, out_shape=jax.ShapeDtypeStruct((groups, ROWS,...]
where the time goes in v3:
time: 66 us; the launch traced here: 66.7 us
  Pallas kernels  62.3 us (94%)
  other arithmetic  2.23 us (3%)
  local copies, waits for them, and re-layouts  1.45 us (2%)
  between operations  0.71 us (1%)
    pallas_call x1, Pallas kernels, filtered_pieces(): pl.pallas_call(functools.partial(filter_kernel, dates, ranges), out_shape...  31.9 us
    pallas_call x1, Pallas kernels, coherence_map(): pl.pallas_call(map_kernel, out_shape=jax.ShapeDtypeStruct((groups, ROWS,...  19.6 us
    pallas_call x1, Pallas kernels, share_from(): pl.pallas_call(functools.partial(share_kernel, owner, dates, ranges), out...  10.8 us
    reshape x2, local copies, waits for them, and re-layouts, filtered_pieces(): weights = gain.reshape(depth, RADIX).T  1.44 us

profile of v3, /device:TPU:3, one launch (start us, length us, event | category | flops | bytes accessed | tf_op | source)
XLA Modules:
  0.0 66.7 jit_solution(9605787011686112612)
XLA Ops:
  0.7 0.8 %fusion.4 = bf16[8,256]{1,0:T(8,128)(2,1)S(1)} fusion(s32[256]{0:T(256)S(1)} %get-tuple-element.63, s32[8]{0:T(128)} %param.22, s32[256]{0:T(256)S(1)} %get-tuple-element.64, s32[8]{0:T(128)} %param.21), kind=kLoop, calls=%fused_computation.8 | loop fusion | flops 34816 | bytes 6208 | tf_op jit(solution)/shard_map/cos | solution.py:50
  1.5 0.8 %fusion.3 = f32[8,256]{1,0:T(8,128)S(1)} fusion(s32[256]{0:T(256)S(1)} %get-tuple-element.63, s32[8]{0:T(128)} %param.22, s32[256]{0:T(256)S(1)} %get-tuple-element.64, s32[8]{0:T(128)} %param.21), kind=kLoop, calls=%fused_computation.7 | loop fusion | flops 32768 | bytes 10304 | tf_op jit(solution)/shard_map/sin | solution.py:51
  2.3 0.6 maximum_convert_fusion.table_ref
  2.9 0.8 %reshape.37 = f32[128,16]{1,0:T(8,128)S(1)} reshape(f32[2048]{0:T(1024)} %param.20) | data formatting | bytes 16384 | tf_op jit(solution)/shard_map/reshape | solution.py:393
  3.7 0.7 %copy.10 = f32[128,16]{0,1:T(8,128)} copy(f32[128,16]{1,0:T(8,128)S(1)} %reshape.37) | data formatting | bytes 16384 | tf_op jit(solution)/shard_map/reshape | solution.py:393
  4.4 10.8 %conditional.1 = ((bf16[2,2048,128]{2,1,0:T(8,128)(2,1)S(1)}, f32[2,8,128]{2,1,0:T(8,128)S(1)})) conditional(s32[]{:T(128)} %bitcast.3, (bf16[2048,128]{1,0:T(8,128)(2,1)}, bf16[2048,128]{1,0:T(8,128)(2,1)}) %tuple.58, (bf16[2048,128]{1,0:T(8,128)(2,1)}, bf16[2048,128]{1,0:T(8,128)(2,1)}) %tuple.59, ...), branch_computations={%region_0.0_spmd, %region_1.0_spmd, %region_2.0_spmd, %region_3.0_... | conditional | bytes 8 | solution.py:280
  4.4 10.8 %share_2.1 = (bf16[2,2048,128]{2,1,0:T(8,128)(2,1)S(1)}, f32[2,8,128]{2,1,0:T(8,128)S(1)}) custom-call(bf16[2048,128]{1,0:T(8,128)(2,1)} %get-tuple-element.41.re_ref, bf16[2048,128]{1,0:T(8,128)(2,1)} %get-tuple-element.42.im_ref), custom_call_target="tpu_custom_call" | custom-call | tf_op jit(solution)/shard_map/cond/branch_2_fun/share_2/pallas_call | solution.py:246
  15.2 31.9 %filter_exchange.1.pieces_ref = bf16[2,8,256,128]{3,2,1,0:T(8,128)(2,1)} custom-call(bf16[2048,128]{1,0:T(8,128)(2,1)} %bitcast.14, bf16[2048,128]{1,0:T(8,128)(2,1)} %bitcast.23, bf16[2,2048,128]{2,1,0:T(8,128)(2,1)S(1)} %get-tuple-element.55.image_ref, f32[2,8,128]{2,1,0:T(8,128)S(1)} %get-tuple-element.56.total_ref, f32[16,128]{1,0:T(8,128)} %bitcast.24, ...), custom_call_target="tpu_custom_call" | custom-call | tf_op jit(solution)/shard_map/filter_exchange/pallas_call | solution.py:395
  47.1 19.6 %coherence_map.1 = f32[16,16,128,256]{3,2,1,0:T(8,128)} custom-call(s32[1]{0:T(128)} %bitcast.index_ref, bf16[2,8,256,128]{3,2,1,0:T(8,128)(2,1)} %filter_exchange.1.pieces_ref, s32[2048,128]{1,0:T(8,128)} %mask_ref.1, f32[16,512]{1,0:T(8,128)} %maximum_convert_fusion.table_ref), custom_call_target="tpu_custom_call" | custom-call | tf_op jit(solution)/shard_map/coherence_map/pallas_call | solution.py:472
  (4 shorter events, 0.0 us)
